TPU v7x, 32 devices: a whole 2x2x4 slice. The times are simulated.
32 devices in a mesh: facet: 8 (over y, x, core), strip: 4 (over z).
Axes of the slice: x: 2, y: 2, z: 4, core: 2. Of those that a mesh axis runs over, the one named last changes fastest.
Arguments:
- facet_pixels: bfloat16 [2, 8, 512, 4096], P(None, 'facet', 'strip'), may hold values from -6 to 6
- facet_offsets: int32 [8, 2], P('facet'), may hold values from 0 to 65535
- subgrid_offsets: int32 [2, 2], replicated, may hold values from 0 to 65023
Outputs:
- subgrid: float32 [512, 2, 2, 512], P('strip', None, None, 'facet')
All inputs are finite; a program needn't handle non-finite values.
Results may differ from a plain program's by a relative error of at most 0.0074.
Values may be sent and summed in bfloat16 or wider, within the bound.
A program may use at most 64 MiB of HBM per device.

v0:
```python
import functools
import math

import jax
import jax.numpy as jnp
import ml_dtypes
import numpy as np
from jax import lax
from jax.experimental import pallas as pl
from jax.experimental.pallas import tpu as pltpu
from jax.sharding import PartitionSpec as P

IMAGE_N = 65536
FREQ = 512
ROW_FREQ = 512
COLUMNS = 2
LANES = 128
CHUNK = 256
BF = jnp.bfloat16
F32 = jnp.float32
MESH = pl.DeviceIdType.MESH


def half_tables(count_a, count_b, step_a):
    a = 2 * np.arange(count_a, dtype=np.int64) + step_a
    b = 2 * np.arange(count_b, dtype=np.int64) + 1
    t = (a[:, None] * b[None, :]) % (4 * IMAGE_N)
    angle = 2.0 * np.pi * t / (4 * IMAGE_N)
    return np.cos(angle), np.sin(angle)


def cos_sin(product, modulus):
    t = (product + modulus // 2) & (modulus - 1)
    h = (t - modulus // 2).astype(F32) * (math.pi / modulus)
    h2 = h * h
    s = jnp.full_like(h, 1.0 / math.factorial(13))
    c = jnp.full_like(h, -1.0 / math.factorial(14))
    for n in range(11, 0, -2):
        s = s * h2 + (-1.0) ** ((n - 1) // 2) / math.factorial(n)
    for n in range(12, -1, -2):
        c = c * h2 + (-1.0) ** (n // 2) / math.factorial(n)
    s = s * h
    return 1.0 - 2.0 * s * s, 2.0 * s * c


def iota(shape, dim):
    return lax.broadcasted_iota(jnp.int32, shape, dim)


def dot(a, b):
    return jnp.dot(a, b, preferred_element_type=F32)


def kernel(
    facets, strips,
    fo_ref, so_ref, x_hbm, ct_hbm, st_hbm, rc_hbm, rs_hbm,
    out_ref,
    x, ct, st, rc, rs, evod, ysend, yrecv, tc, ts, off_send, off_recv, zsend, zrecv,
    load_sem, y_ssem, y_rsem, o_ssem, o_rsem, z_ssem, z_rsem,
):
    f_me = lax.axis_index("facet")
    s_me = lax.axis_index("strip")
    rows, width = x.shape[1], x.shape[2]
    half_k = width // 2
    half_m = FREQ // 2
    half_i = ROW_FREQ // 2
    mb = FREQ // facets
    ib = ROW_FREQ // strips
    chunks = half_k // CHUNK
    scale = 1.0 / math.sqrt(width * rows * strips * facets)

    loads = []

    def load(src, dst):
        copy = pltpu.make_async_copy(src, dst, load_sem.at[len(loads)])
        copy.start()
        loads.append(copy)
        return copy

    x_low, x_high = [], []
    for j in range(chunks):
        low = pl.ds((chunks - 1 - j) * CHUNK, CHUNK)
        high = pl.ds(half_k + j * CHUNK, CHUNK)
        x_low.append(load(x_hbm.at[:, 0, :, low], x.at[:, :, low]))
        x_high.append(load(x_hbm.at[:, 0, :, high], x.at[:, :, high]))
    ct_load = load(ct_hbm, ct)
    st_load = load(st_hbm, st)
    rc_load = load(rc_hbm, rc)
    rs_load = load(rs_hbm, rs)

    facet_peers = [lax.rem(f_me + d, facets) for d in range(1, facets)]
    strip_peers = [lax.rem(s_me + d, strips) for d in range(1, strips)]
    barrier = pltpu.get_barrier_semaphore()
    for peer in facet_peers:
        pl.semaphore_signal(barrier, inc=1, device_id=(peer, s_me), device_id_type=MESH)
    for peer in strip_peers:
        pl.semaphore_signal(barrier, inc=1, device_id=(f_me, peer), device_id_type=MESH)

    fx = fo_ref[0, 0]
    fy = fo_ref[0, 1]
    u0 = [so_ref[c, 0] for c in range(COLUMNS)]
    w0 = [so_ref[c, 1] for c in range(COLUMNS)]

    off_send[...] = jnp.full(off_send.shape, fy, jnp.int32)
    off_recv[f_me] = off_send[...]

    pieces = half_k // LANES
    a_index = iota((pieces, LANES), 0) * LANES + iota((pieces, LANES), 1)
    pq = [
        cos_sin((2 * a_index + 1) * (2 * u0[c] + (FREQ - 1)), 4 * IMAGE_N)
        for c in range(COLUMNS)
    ]

    row = iota((8, half_m), 0)
    lane = iota((8, half_m), 1)
    first = jnp.where(row < 2, u0[0], u0[1])
    freq = first + jnp.where((row & 1) == 0, half_m + lane, half_m - 1 - lane)
    hc, hs = cos_sin((2 * fx + (width - 1)) * freq, 2 * IMAGE_N)
    hc, hs = hc * scale, hs * scale

    padded = -(-rows // LANES) * LANES
    row = iota((8, padded), 0)
    first = jnp.where(row == 0, w0[0], w0[1])
    pixel_row = s_me * rows + iota((8, padded), 1) + fy
    gc, gs = cos_sin((2 * first + (ROW_FREQ - 1)) * pixel_row, 2 * IMAGE_N)
    gc, gs = jnp.transpose(gc), jnp.transpose(gs)

    flip = (iota((CHUNK, CHUNK), 0) + iota((CHUNK, CHUNK), 1) == CHUNK - 1).astype(F32).astype(BF)

    for j in range(chunks):
        cols = pl.ds(j * CHUNK, CHUNK)
        x_low[j].wait()
        x_high[j].wait()
        low = x[:, :, pl.ds((chunks - 1 - j) * CHUNK, CHUNK)].reshape(2 * rows, CHUNK)
        high = x[:, :, pl.ds(half_k + j * CHUNK, CHUNK)].reshape(2 * rows, CHUNK).astype(F32)
        low = dot(low, flip)
        even = high + low
        odd = high - low
        er, ei, odr, odi = even[:rows], even[rows:], odd[:rows], odd[rows:]
        first = j * (CHUNK // LANES)
        for c in range(COLUMNS):
            p, q = (
                jnp.concatenate(
                    [part[first + n : first + n + 1] for n in range(CHUNK // LANES)], axis=1
                )
                for part in pq[c]
            )
            evod[c, 0, :rows, cols] = (er * p + odi * q).astype(BF)
            evod[c, 0, rows:, cols] = (ei * p - odr * q).astype(BF)
            evod[c, 1, :rows, cols] = (odr * p + ei * q).astype(BF)
            evod[c, 1, rows:, cols] = (odi * p - er * q).astype(BF)

    pl.semaphore_wait(barrier, facets - 1 + strips - 1)

    def off_copy(d):
        return pltpu.make_async_remote_copy(
            src_ref=off_send,
            dst_ref=off_recv.at[f_me],
            send_sem=o_ssem.at[d - 1],
            recv_sem=o_rsem.at[d - 1],
            device_id=(facet_peers[d - 1], s_me),
            device_id_type=MESH,
        )

    def y_copy(c, d):
        return pltpu.make_async_remote_copy(
            src_ref=ysend.at[c, facet_peers[d - 1]],
            dst_ref=yrecv.at[c, f_me],
            send_sem=y_ssem.at[c, d - 1],
            recv_sem=y_rsem.at[c, d - 1],
            device_id=(facet_peers[d - 1], s_me),
            device_id_type=MESH,
        )

    def z_copy(c, d):
        return pltpu.make_async_remote_copy(
            src_ref=zsend.at[c, strip_peers[d - 1]],
            dst_ref=zrecv.at[c, d - 1],
            send_sem=z_ssem.at[c, d - 1],
            recv_sem=z_rsem.at[c, d - 1],
            device_id=(f_me, strip_peers[d - 1]),
            device_id_type=MESH,
        )

    off_copies = [off_copy(d) for d in range(1, facets)]
    for copy in off_copies:
        copy.start()

    ct_load.wait()
    st_load.wait()
    y_copies = []
    for c in range(COLUMNS):
        pp = dot(evod[c, 0], ct[...])
        qq = dot(evod[c, 1], st[...])
        halves = []
        for sign in (0, 1):
            if sign == 0:
                yr = pp[:rows] + qq[rows:]
                yi = pp[rows:] - qq[:rows]
            else:
                yr = pp[:rows] - qq[rows:]
                yi = pp[rows:] + qq[:rows]
            hcr, hsr = hc[2 * c + sign : 2 * c + sign + 1], hs[2 * c + sign : 2 * c + sign + 1]
            gcr, gsr = gc[:rows, c : c + 1], gs[:rows, c : c + 1]
            a = gcr * hcr - gsr * hsr
            b = gcr * hsr + gsr * hcr
            halves.append(((yr * a + yi * b).astype(BF), (yi * a - yr * b).astype(BF)))
        for f in range(facets):
            if f >= facets // 2:
                yr, yi = halves[0]
                start = mb * f - half_m
            else:
                yr, yi = halves[1]
                start = half_m - mb * (f + 1)
            ysend[c, f] = jnp.concatenate(
                [yr[:, start : start + mb], yi[:, start : start + mb]], axis=1
            )
        copies = [y_copy(c, d) for d in range(1, facets)]
        for copy in copies:
            copy.start()
        y_copies.append(copies)
        yrecv[c, f_me] = ysend[c, f_me]

    for copy in off_copies:
        copy.wait_recv()
    rc_load.wait()
    rs_load.wait()
    offs = jnp.concatenate([off_recv[:, 0, :]] * (half_i // LANES), axis=1)
    phc, phs = cos_sin(
        (2 * iota((facets, half_i), 1) + 1) * (offs + s_me * rows), 2 * IMAGE_N
    )
    phc, phs = jnp.transpose(phc), jnp.transpose(phs)
    base_c, base_s = rc[...], rs[...]
    for f in range(facets):
        pc, ps = phc[:, f : f + 1], phs[:, f : f + 1]
        tc[:, f * rows : (f + 1) * rows] = (base_c * pc - base_s * ps).astype(BF)
        ts[:, f * rows : (f + 1) * rows] = (base_s * pc + base_c * ps).astype(BF)

    src, dst = iota((2 * mb, 2 * mb), 0), iota((2 * mb, 2 * mb), 1)
    same_part = (src >= mb) == (dst >= mb)
    mirrored = (src + dst - jnp.where(dst >= mb, 2 * mb, 0)) == mb - 1
    lower = jnp.where(f_me < facets // 2, 1, 0)
    picked = jnp.where(lower == 1, jnp.where(same_part & mirrored, 1, 0), jnp.where(src == dst, 1, 0))
    order = picked.astype(F32).astype(BF)

    z_copies = []
    for c in range(COLUMNS):
        for copy in y_copies[c]:
            copy.wait_recv()
        y = yrecv[c].reshape(facets * rows, 2 * mb)
        aa = dot(tc[...], y)
        bb = dot(ts[...], y)
        turned = jnp.concatenate([bb[:, mb:], -bb[:, :mb]], axis=1)
        upper_rows = dot((aa + turned).astype(BF), order).astype(BF)
        lower_rows = dot(flip, (aa - turned).astype(BF)).astype(BF)
        lower_rows = dot(lower_rows, order).astype(BF)
        z = jnp.concatenate([lower_rows, upper_rows], axis=0)
        zsend[c] = z.reshape(strips, ib, 2 * mb)
        copies = [z_copy(c, d) for d in range(1, strips)]
        for copy in copies:
            copy.start()
        z_copies.append(copies)

    totals = []
    for c in range(COLUMNS):
        total = zsend[c, s_me].astype(F32)
        for d in range(1, strips):
            z_copies[c][d - 1].wait_recv()
            total += zrecv[c, d - 1].astype(F32)
        totals.append(total)
    out_ref[...] = jnp.concatenate(
        [totals[0][:, :mb], totals[1][:, :mb], totals[0][:, mb:], totals[1][:, mb:]], axis=1
    )
    for copy in off_copies + y_copies[0] + y_copies[1] + z_copies[0] + z_copies[1]:
        copy.wait_send()


def per_device(facet_pixels, facet_offsets, subgrid_offsets):
    rows, width = facet_pixels.shape[2], facet_pixels.shape[3]
    facets, strips = lax.axis_size("facet"), lax.axis_size("strip")
    mb, ib = FREQ // facets, ROW_FREQ // strips
    half_k, half_m, half_i = width // 2, FREQ // 2, ROW_FREQ // 2
    ct, st = (t.astype(ml_dtypes.bfloat16) for t in half_tables(half_k, half_m, 1))
    rc, rs = (
        np.ascontiguousarray(t.T.astype(np.float32)) for t in half_tables_rows(rows, half_i)
    )
    loads = 2 * (half_k // CHUNK) + 4
    dma = pltpu.SemaphoreType.DMA
    flops = 2 * (4 * 2 * rows * half_k * half_m + 4 * half_i * facets * rows * 2 * mb)
    out = pl.pallas_call(
        functools.partial(kernel, facets, strips),
        out_shape=jax.ShapeDtypeStruct((ib, 4 * mb), F32),
        in_specs=[pl.BlockSpec(memory_space=pltpu.SMEM)] * 2
        + [pl.BlockSpec(memory_space=pl.ANY)] * 5,
        out_specs=pl.BlockSpec(memory_space=pltpu.VMEM),
        scratch_shapes=[
            pltpu.VMEM((2, rows, width), BF),
            pltpu.VMEM((half_k, half_m), BF),
            pltpu.VMEM((half_k, half_m), BF),
            pltpu.VMEM((half_i, rows), F32),
            pltpu.VMEM((half_i, rows), F32),
            pltpu.VMEM((COLUMNS, 2, 2 * rows, half_k), BF),
            pltpu.VMEM((COLUMNS, facets, rows, 2 * mb), BF),
            pltpu.VMEM((COLUMNS, facets, rows, 2 * mb), BF),
            pltpu.VMEM((half_i, facets * rows), BF),
            pltpu.VMEM((half_i, facets * rows), BF),
            pltpu.VMEM((8, LANES), jnp.int32),
            pltpu.VMEM((facets, 8, LANES), jnp.int32),
            pltpu.VMEM((COLUMNS, strips, ib, 2 * mb), BF),
            pltpu.VMEM((COLUMNS, strips - 1, ib, 2 * mb), BF),
            dma((loads,)),
            dma((COLUMNS, facets - 1)),
            dma((COLUMNS, facets - 1)),
            dma((facets - 1,)),
            dma((facets - 1,)),
            dma((COLUMNS, strips - 1)),
            dma((COLUMNS, strips - 1)),
        ],
        compiler_params=pltpu.CompilerParams(
            collective_id=0, has_side_effects=True, vmem_limit_bytes=40 * 1024 * 1024
        ),
        cost_estimate=pl.CostEstimate(
            flops=flops, bytes_accessed=4 * 1024 * 1024, transcendentals=0
        ),
    )(facet_offsets, subgrid_offsets, facet_pixels, ct, st, rc, rs)
    return out.reshape(ib, 2, COLUMNS, mb)


def half_tables_rows(rows, half_i):
    r = np.arange(rows, dtype=np.int64)
    b = 2 * np.arange(half_i, dtype=np.int64) + 1
    t = (r[:, None] * b[None, :]) % (2 * IMAGE_N)
    angle = 2.0 * np.pi * t / (2 * IMAGE_N)
    return np.cos(angle), np.sin(angle)


def solution(mesh):
    in_specs = (P(None, "facet", "strip", None), P("facet", None), P())
    out_specs = P("strip", None, None, "facet")
    return jax.shard_map(
        per_device, mesh=mesh, in_specs=in_specs, out_specs=out_specs, check_vma=False
    )
```

profile of v0, /device:TPU:0, one launch (start us, length us, event | category | flops | bytes accessed | tf_op | source)
XLA Modules:
  0.0 29.4 jit_solution(133547843805363130)
XLA Ops:
  0.0 0.0 copy-start
  0.0 1.6 %copy-done = bf16[2,1,128,4096]{3,2,1,0:T(8,128)(2,1)S(1)} copy-done((bf16[2,1,128,4096]{3,2,1,0:T(8,128)(2,1)S(1)}, bf16[2,1,128,4096]{3,2,1,0:T(8,128)(2,1)}, u32[]{:S(2)}) %copy-start) | copy-done | bytes 2097176
  1.6 0.0 copy-start.1
  1.6 0.7 %copy-done.1 = s32[2,2]{1,0:T(2,128)S(1)} copy-done((s32[2,2]{1,0:T(2,128)S(1)}, s32[2,2]{1,0:T(2,128)}, u32[]{:S(2)}) %copy-start.1) | copy-done | bytes 40
  2.3 0.0 copy-start.2
  2.3 0.7 %copy-done.2 = s32[1,2]{1,0:T(1,128)S(1)} copy-done((s32[1,2]{1,0:T(1,128)S(1)}, s32[1,2]{1,0:T(1,128)}, u32[]{:S(2)}) %copy-start.2) | copy-done | bytes 32
  2.9 0.0 copy-start.3
  2.9 1.2 %copy-done.3 = bf16[2048,256]{1,0:T(8,128)(2,1)S(1)} copy-done((bf16[2048,256]{1,0:T(8,128)(2,1)S(1)}, bf16[2048,256]{1,0:T(8,128)(2,1)}, u32[]{:S(2)}) %copy-start.3) | copy-done | bytes 1048600
  4.2 0.0 copy-start.4
  4.2 1.2 %copy-done.4 = bf16[2048,256]{1,0:T(8,128)(2,1)S(1)} copy-done((bf16[2048,256]{1,0:T(8,128)(2,1)S(1)}, bf16[2048,256]{1,0:T(8,128)(2,1)}, u32[]{:S(2)}) %copy-start.4) | copy-done | bytes 1048600
  5.4 0.0 copy-start.5
  5.4 0.9 %copy-done.5 = f32[256,128]{1,0:T(8,128)S(1)} copy-done((f32[256,128]{1,0:T(8,128)S(1)}, f32[256,128]{1,0:T(8,128)}, u32[]{:S(2)}) %copy-start.5) | copy-done | bytes 131096
  6.3 0.0 copy-start.6
  6.3 0.9 %copy-done.6 = f32[256,128]{1,0:T(8,128)S(1)} copy-done((f32[256,128]{1,0:T(8,128)S(1)}, f32[256,128]{1,0:T(8,128)}, u32[]{:S(2)}) %copy-start.6) | copy-done | bytes 131096
  7.2 21.4 %shard_map.73 = f32[128,256]{1,0:T(8,128)S(1)} custom-call(s32[1,2]{1,0:T(1,128)S(1)} %copy-done.2, s32[2,2]{1,0:T(2,128)S(1)} %copy-done.1, bf16[2,1,128,4096]{3,2,1,0:T(8,128)(2,1)S(1)} %copy-done, bf16[2048,256]{1,0:T(8,128)(2,1)S(1)} %copy-done.4, bf16[2048,256]{1,0:T(8,128)(2,1)S(1)} %copy-done.3, f32[256,128]{1,0:T(8,128)S(1)} %copy-done.6, ...), custom_call_target="tpu_custom_call" | custom-call | flops 1342177280 | bytes 4194304 | tf_op jit(solution)/shard_map/pallas_call | solution.py:290
  28.6 0.8 %copy.9 = f32[128,256]{0,1:T(8,128)} copy(f32[128,256]{1,0:T(8,128)S(1)} %shard_map.73) | data formatting | bytes 262144 | tf_op jit(solution)/shard_map/pallas_call | solution.py:290
Async XLA Ops:
  0.0 1.6 %copy-start = (bf16[2,1,128,4096]{3,2,1,0:T(8,128)(2,1)S(1)}, bf16[2,1,128,4096]{3,2,1,0:T(8,128)(2,1)}, u32[]{:S(2)}) copy-start(bf16[2,1,128,4096]{3,2,1,0:T(8,128)(2,1)} %x_hbm.1) | copy-start | bytes 6291460
  1.6 0.7 %copy-start.1 = (s32[2,2]{1,0:T(2,128)S(1)}, s32[2,2]{1,0:T(2,128)}, u32[]{:S(2)}) copy-start(s32[2,2]{1,0:T(2,128)} %so_ref.1) | copy-start | bytes 52
  2.3 0.7 %copy-start.2 = (s32[1,2]{1,0:T(1,128)S(1)}, s32[1,2]{1,0:T(1,128)}, u32[]{:S(2)}) copy-start(s32[1,2]{1,0:T(1,128)} %fo_ref.1) | copy-start | bytes 28
  2.9 1.2 %copy-start.3 = (bf16[2048,256]{1,0:T(8,128)(2,1)S(1)}, bf16[2048,256]{1,0:T(8,128)(2,1)}, u32[]{:S(2)}) copy-start(bf16[2048,256]{1,0:T(8,128)(2,1)} %constant.9.clone.st_hbm) | copy-start | bytes 3145732
  4.2 1.2 %copy-start.4 = (bf16[2048,256]{1,0:T(8,128)(2,1)S(1)}, bf16[2048,256]{1,0:T(8,128)(2,1)}, u32[]{:S(2)}) copy-start(bf16[2048,256]{1,0:T(8,128)(2,1)} %constant.8.clone.ct_hbm) | copy-start | bytes 3145732
  5.4 0.9 %copy-start.5 = (f32[256,128]{1,0:T(8,128)S(1)}, f32[256,128]{1,0:T(8,128)}, u32[]{:S(2)}) copy-start(f32[256,128]{1,0:T(8,128)} %constant.11.clone.rs_hbm) | copy-start | bytes 393220
  6.3 0.9 %copy-start.6 = (f32[256,128]{1,0:T(8,128)S(1)}, f32[256,128]{1,0:T(8,128)}, u32[]{:S(2)}) copy-start(f32[256,128]{1,0:T(8,128)} %constant.10.clone.rc_hbm) | copy-start | bytes 393220
where the time goes:
time: 29.8 us; the launch traced here: 29.4 us
  Pallas kernels  21.4 us (72%)
  local copies, waits for them, and re-layouts  7.94 us (27%)
    pallas_call x1, Pallas kernels, per_device(): pl.pallas_call(functools.partial(kernel, facets, strips), out_shape=jax.S...  21.4 us
    unnamed x14, local copies, waits for them, and re-layouts  7.18 us
    pallas_call x1, local copies, waits for them, and re-layouts, per_device(): pl.pallas_call(functools.partial(kernel, facets, strips), out_shape=jax.S...  0.76 us

commit v1 on v0

--- a/solution.py
+++ b/solution.py
@@ -53,9 +53,9 @@
 
 def kernel(
     facets, strips,
-    fo_ref, so_ref, x_hbm, ct_hbm, st_hbm, rc_hbm, rs_hbm,
+    fo_hbm, so_hbm, x_hbm, ct_hbm, st_hbm, rc_hbm, rs_hbm,
     out_ref,
-    x, ct, st, rc, rs, evod, ysend, yrecv, tc, ts, off_send, off_recv, zsend, zrecv,
+    fo_ref, so_ref, x, ct, st, rc, rs, evod, ysend, yrecv, tc, ts, off_send, off_recv, zsend, zrecv,
     load_sem, y_ssem, y_rsem, o_ssem, o_rsem, z_ssem, z_rsem,
 ):
     f_me = lax.axis_index("facet")
@@ -77,6 +77,8 @@
         loads.append(copy)
         return copy
 
+    fo_load = load(fo_hbm, fo_ref)
+    so_load = load(so_hbm, so_ref)
     x_low, x_high = [], []
     for j in range(chunks):
         low = pl.ds((chunks - 1 - j) * CHUNK, CHUNK)
@@ -96,6 +98,8 @@
     for peer in strip_peers:
         pl.semaphore_signal(barrier, inc=1, device_id=(f_me, peer), device_id_type=MESH)
 
+    fo_load.wait()
+    so_load.wait()
     fx = fo_ref[0, 0]
     fy = fo_ref[0, 1]
     u0 = [so_ref[c, 0] for c in range(COLUMNS)]
@@ -127,18 +131,19 @@
 
     flip = (iota((CHUNK, CHUNK), 0) + iota((CHUNK, CHUNK), 1) == CHUNK - 1).astype(F32).astype(BF)
 
-    for j in range(chunks):
-        cols = pl.ds(j * CHUNK, CHUNK)
-        x_low[j].wait()
-        x_high[j].wait()
-        low = x[:, :, pl.ds((chunks - 1 - j) * CHUNK, CHUNK)].reshape(2 * rows, CHUNK)
-        high = x[:, :, pl.ds(half_k + j * CHUNK, CHUNK)].reshape(2 * rows, CHUNK).astype(F32)
-        low = dot(low, flip)
-        even = high + low
-        odd = high - low
-        er, ei, odr, odi = even[:rows], even[rows:], odd[:rows], odd[rows:]
-        first = j * (CHUNK // LANES)
-        for c in range(COLUMNS):
+    def phase_column(c):
+        for j in range(chunks):
+            cols = pl.ds(j * CHUNK, CHUNK)
+            if c == 0:
+                x_low[j].wait()
+                x_high[j].wait()
+            low = x[:, :, pl.ds((chunks - 1 - j) * CHUNK, CHUNK)].reshape(2 * rows, CHUNK)
+            high = x[:, :, pl.ds(half_k + j * CHUNK, CHUNK)].reshape(2 * rows, CHUNK).astype(F32)
+            low = dot(low, flip)
+            even = high + low
+            odd = high - low
+            er, ei, odr, odi = even[:rows], even[rows:], odd[:rows], odd[rows:]
+            first = j * (CHUNK // LANES)
             p, q = (
                 jnp.concatenate(
                     [part[first + n : first + n + 1] for n in range(CHUNK // LANES)], axis=1
@@ -150,6 +155,7 @@
             evod[c, 1, :rows, cols] = (odr * p + ei * q).astype(BF)
             evod[c, 1, rows:, cols] = (odi * p - er * q).astype(BF)
 
+    phase_column(0)
     pl.semaphore_wait(barrier, facets - 1 + strips - 1)
 
     def off_copy(d):
@@ -186,10 +192,13 @@
     for copy in off_copies:
         copy.start()
 
-    ct_load.wait()
-    st_load.wait()
     y_copies = []
     for c in range(COLUMNS):
+        if c > 0:
+            phase_column(c)
+        else:
+            ct_load.wait()
+            st_load.wait()
         pp = dot(evod[c, 0], ct[...])
         qq = dot(evod[c, 1], st[...])
         halves = []
@@ -284,16 +293,17 @@
     rc, rs = (
         np.ascontiguousarray(t.T.astype(np.float32)) for t in half_tables_rows(rows, half_i)
     )
-    loads = 2 * (half_k // CHUNK) + 4
+    loads = 2 * (half_k // CHUNK) + 6
     dma = pltpu.SemaphoreType.DMA
     flops = 2 * (4 * 2 * rows * half_k * half_m + 4 * half_i * facets * rows * 2 * mb)
     out = pl.pallas_call(
         functools.partial(kernel, facets, strips),
         out_shape=jax.ShapeDtypeStruct((ib, 4 * mb), F32),
-        in_specs=[pl.BlockSpec(memory_space=pltpu.SMEM)] * 2
-        + [pl.BlockSpec(memory_space=pl.ANY)] * 5,
+        in_specs=[pl.BlockSpec(memory_space=pltpu.HBM)] * 7,
         out_specs=pl.BlockSpec(memory_space=pltpu.VMEM),
         scratch_shapes=[
+            pltpu.SMEM((1, 2), jnp.int32),
+            pltpu.SMEM((COLUMNS, 2), jnp.int32),
             pltpu.VMEM((2, rows, width), BF),
             pltpu.VMEM((half_k, half_m), BF),
             pltpu.VMEM((half_k, half_m), BF),

time: 29.8 us -> 29.2 us (0.980)
  Pallas kernels: 21.4 us -> 21 us
    pallas_call x1, Pallas kernels: 21.4 us -> 21 us  [per_device(): pl.pallas_call(functools.partial(kernel, facets, strips), out_shape=jax.S...]
where the time goes in v1:
time: 29.2 us; the launch traced here: 29 us
  Pallas kernels  21 us (72%)
  local copies, waits for them, and re-layouts  7.94 us (27%)
    pallas_call x1, Pallas kernels, per_device(): pl.pallas_call(functools.partial(kernel, facets, strips), out_shape=jax.S...  21 us
    unnamed x14, local copies, waits for them, and re-layouts  7.18 us
    pallas_call x1, local copies, waits for them, and re-layouts, per_device(): pl.pallas_call(functools.partial(kernel, facets, strips), out_shape=jax.S...  0.76 us

profile of v1, /device:TPU:0, one launch (start us, length us, event | category | flops | bytes accessed | tf_op | source)
XLA Modules:
  0.0 29.0 jit_solution(560500459615119446)
XLA Ops:
  0.0 0.0 copy-start
  0.0 1.6 %copy-done = bf16[2,1,128,4096]{3,2,1,0:T(8,128)(2,1)S(1)} copy-done((bf16[2,1,128,4096]{3,2,1,0:T(8,128)(2,1)S(1)}, bf16[2,1,128,4096]{3,2,1,0:T(8,128)(2,1)}, u32[]{:S(2)}) %copy-start) | copy-done | bytes 2097176
  1.6 0.0 copy-start.1
  1.6 0.7 %copy-done.1 = s32[2,2]{1,0:T(2,128)S(1)} copy-done((s32[2,2]{1,0:T(2,128)S(1)}, s32[2,2]{1,0:T(2,128)}, u32[]{:S(2)}) %copy-start.1) | copy-done | bytes 40
  2.3 0.0 copy-start.2
  2.3 0.7 %copy-done.2 = s32[1,2]{1,0:T(1,128)S(1)} copy-done((s32[1,2]{1,0:T(1,128)S(1)}, s32[1,2]{1,0:T(1,128)}, u32[]{:S(2)}) %copy-start.2) | copy-done | bytes 32
  2.9 0.0 copy-start.3
  2.9 1.2 %copy-done.3 = bf16[2048,256]{1,0:T(8,128)(2,1)S(1)} copy-done((bf16[2048,256]{1,0:T(8,128)(2,1)S(1)}, bf16[2048,256]{1,0:T(8,128)(2,1)}, u32[]{:S(2)}) %copy-start.3) | copy-done | bytes 1048600
  4.2 0.0 copy-start.4
  4.2 1.2 %copy-done.4 = bf16[2048,256]{1,0:T(8,128)(2,1)S(1)} copy-done((bf16[2048,256]{1,0:T(8,128)(2,1)S(1)}, bf16[2048,256]{1,0:T(8,128)(2,1)}, u32[]{:S(2)}) %copy-start.4) | copy-done | bytes 1048600
  5.4 0.0 copy-start.5
  5.4 0.9 %copy-done.5 = f32[256,128]{1,0:T(8,128)S(1)} copy-done((f32[256,128]{1,0:T(8,128)S(1)}, f32[256,128]{1,0:T(8,128)}, u32[]{:S(2)}) %copy-start.5) | copy-done | bytes 131096
  6.3 0.0 copy-start.6
  6.3 0.9 %copy-done.6 = f32[256,128]{1,0:T(8,128)S(1)} copy-done((f32[256,128]{1,0:T(8,128)S(1)}, f32[256,128]{1,0:T(8,128)}, u32[]{:S(2)}) %copy-start.6) | copy-done | bytes 131096
  7.2 21.0 %shard_map.73 = f32[128,256]{1,0:T(8,128)S(1)} custom-call(s32[1,2]{1,0:T(1,128)S(1)} %copy-done.2, s32[2,2]{1,0:T(2,128)S(1)} %copy-done.1, bf16[2,1,128,4096]{3,2,1,0:T(8,128)(2,1)S(1)} %copy-done, bf16[2048,256]{1,0:T(8,128)(2,1)S(1)} %copy-done.4, bf16[2048,256]{1,0:T(8,128)(2,1)S(1)} %copy-done.3, f32[256,128]{1,0:T(8,128)S(1)} %copy-done.6, ...), custom_call_target="tpu_custom_call" | custom-call | flops 1342177280 | bytes 4194304 | tf_op jit(solution)/shard_map/pallas_call | solution.py:299
  28.2 0.8 %copy.9 = f32[128,256]{0,1:T(8,128)} copy(f32[128,256]{1,0:T(8,128)S(1)} %shard_map.73) | data formatting | bytes 262144 | tf_op jit(solution)/shard_map/pallas_call | solution.py:299
Async XLA Ops:
  0.0 1.6 %copy-start = (bf16[2,1,128,4096]{3,2,1,0:T(8,128)(2,1)S(1)}, bf16[2,1,128,4096]{3,2,1,0:T(8,128)(2,1)}, u32[]{:S(2)}) copy-start(bf16[2,1,128,4096]{3,2,1,0:T(8,128)(2,1)} %x_hbm.1) | copy-start | bytes 6291460
  1.6 0.7 %copy-start.1 = (s32[2,2]{1,0:T(2,128)S(1)}, s32[2,2]{1,0:T(2,128)}, u32[]{:S(2)}) copy-start(s32[2,2]{1,0:T(2,128)} %so_hbm.1) | copy-start | bytes 52
  2.3 0.7 %copy-start.2 = (s32[1,2]{1,0:T(1,128)S(1)}, s32[1,2]{1,0:T(1,128)}, u32[]{:S(2)}) copy-start(s32[1,2]{1,0:T(1,128)} %fo_hbm.1) | copy-start | bytes 28
  2.9 1.2 %copy-start.3 = (bf16[2048,256]{1,0:T(8,128)(2,1)S(1)}, bf16[2048,256]{1,0:T(8,128)(2,1)}, u32[]{:S(2)}) copy-start(bf16[2048,256]{1,0:T(8,128)(2,1)} %constant.9.clone.st_hbm) | copy-start | bytes 3145732
  4.2 1.2 %copy-start.4 = (bf16[2048,256]{1,0:T(8,128)(2,1)S(1)}, bf16[2048,256]{1,0:T(8,128)(2,1)}, u32[]{:S(2)}) copy-start(bf16[2048,256]{1,0:T(8,128)(2,1)} %constant.8.clone.ct_hbm) | copy-start | bytes 3145732
  5.4 0.9 %copy-start.5 = (f32[256,128]{1,0:T(8,128)S(1)}, f32[256,128]{1,0:T(8,128)}, u32[]{:S(2)}) copy-start(f32[256,128]{1,0:T(8,128)} %constant.11.clone.rs_hbm) | copy-start | bytes 393220
  6.3 0.9 %copy-start.6 = (f32[256,128]{1,0:T(8,128)S(1)}, f32[256,128]{1,0:T(8,128)}, u32[]{:S(2)}) copy-start(f32[256,128]{1,0:T(8,128)} %constant.10.clone.rc_hbm) | copy-start | bytes 393220

commit v2 on v1

--- a/solution.py
+++ b/solution.py
@@ -16,6 +16,7 @@
 COLUMNS = 2
 LANES = 128
 CHUNK = 256
+BLOCK = 16
 BF = jnp.bfloat16
 F32 = jnp.float32
 MESH = pl.DeviceIdType.MESH
@@ -55,7 +56,7 @@
     facets, strips,
     fo_hbm, so_hbm, x_hbm, ct_hbm, st_hbm, rc_hbm, rs_hbm,
     out_ref,
-    fo_ref, so_ref, x, ct, st, rc, rs, evod, ysend, yrecv, tc, ts, off_send, off_recv, zsend, zrecv,
+    fo_ref, so_ref, x, xr, ct, st, rc, rs, evod, gc_ref, gs_ref, pp, qq, ysend, yrecv, tc, ts, off_send, off_recv, zsend, zrecv,
     load_sem, y_ssem, y_rsem, o_ssem, o_rsem, z_ssem, z_rsem,
 ):
     f_me = lax.axis_index("facet")
@@ -127,22 +128,26 @@
     first = jnp.where(row == 0, w0[0], w0[1])
     pixel_row = s_me * rows + iota((8, padded), 1) + fy
     gc, gs = cos_sin((2 * first + (ROW_FREQ - 1)) * pixel_row, 2 * IMAGE_N)
-    gc, gs = jnp.transpose(gc), jnp.transpose(gs)
+    gc_ref[...] = jnp.transpose(gc)
+    gs_ref[...] = jnp.transpose(gs)
 
     flip = (iota((CHUNK, CHUNK), 0) + iota((CHUNK, CHUNK), 1) == CHUNK - 1).astype(F32).astype(BF)
+
+    def row_block(n):
+        return pl.ds(pl.multiple_of(n * BLOCK, BLOCK), BLOCK)
+
+    def im_block(n):
+        return pl.ds(pl.multiple_of(rows + n * BLOCK, BLOCK), BLOCK)
 
     def phase_column(c):
         for j in range(chunks):
             cols = pl.ds(j * CHUNK, CHUNK)
+            high_cols = pl.ds(half_k + j * CHUNK, CHUNK)
             if c == 0:
                 x_low[j].wait()
                 x_high[j].wait()
-            low = x[:, :, pl.ds((chunks - 1 - j) * CHUNK, CHUNK)].reshape(2 * rows, CHUNK)
-            high = x[:, :, pl.ds(half_k + j * CHUNK, CHUNK)].reshape(2 * rows, CHUNK).astype(F32)
-            low = dot(low, flip)
-            even = high + low
-            odd = high - low
-            er, ei, odr, odi = even[:rows], even[rows:], odd[:rows], odd[rows:]
+                low = x[:, :, pl.ds((chunks - 1 - j) * CHUNK, CHUNK)].reshape(2 * rows, CHUNK)
+                xr[:, cols] = dot(low, flip).astype(BF)
             first = j * (CHUNK // LANES)
             p, q = (
                 jnp.concatenate(
@@ -150,10 +155,19 @@
                 )
                 for part in pq[c]
             )
-            evod[c, 0, :rows, cols] = (er * p + odi * q).astype(BF)
-            evod[c, 0, rows:, cols] = (ei * p - odr * q).astype(BF)
-            evod[c, 1, :rows, cols] = (odr * p + ei * q).astype(BF)
-            evod[c, 1, rows:, cols] = (odi * p - er * q).astype(BF)
+
+            def block(n, carry):
+                re, im = row_block(n), im_block(n)
+                hr, hi = x[0, re, high_cols].astype(F32), x[1, re, high_cols].astype(F32)
+                lr, li = xr[re, cols].astype(F32), xr[im, cols].astype(F32)
+                er, odr, ei, odi = hr + lr, hr - lr, hi + li, hi - li
+                evod[c, 0, re, cols] = (er * p + odi * q).astype(BF)
+                evod[c, 0, im, cols] = (ei * p - odr * q).astype(BF)
+                evod[c, 1, re, cols] = (odr * p + ei * q).astype(BF)
+                evod[c, 1, im, cols] = (odi * p - er * q).astype(BF)
+                return carry
+
+            lax.fori_loop(0, rows // BLOCK, block, 0, unroll=True)
 
     phase_column(0)
     pl.semaphore_wait(barrier, facets - 1 + strips - 1)
@@ -199,31 +213,33 @@
         else:
             ct_load.wait()
             st_load.wait()
-        pp = dot(evod[c, 0], ct[...])
-        qq = dot(evod[c, 1], st[...])
-        halves = []
-        for sign in (0, 1):
-            if sign == 0:
-                yr = pp[:rows] + qq[rows:]
-                yi = pp[rows:] - qq[:rows]
-            else:
-                yr = pp[:rows] - qq[rows:]
-                yi = pp[rows:] + qq[:rows]
-            hcr, hsr = hc[2 * c + sign : 2 * c + sign + 1], hs[2 * c + sign : 2 * c + sign + 1]
-            gcr, gsr = gc[:rows, c : c + 1], gs[:rows, c : c + 1]
-            a = gcr * hcr - gsr * hsr
-            b = gcr * hsr + gsr * hcr
-            halves.append(((yr * a + yi * b).astype(BF), (yi * a - yr * b).astype(BF)))
-        for f in range(facets):
-            if f >= facets // 2:
-                yr, yi = halves[0]
-                start = mb * f - half_m
-            else:
-                yr, yi = halves[1]
-                start = half_m - mb * (f + 1)
-            ysend[c, f] = jnp.concatenate(
-                [yr[:, start : start + mb], yi[:, start : start + mb]], axis=1
-            )
+        pp[...] = dot(evod[c, 0], ct[...])
+        qq[...] = dot(evod[c, 1], st[...])
+
+        def block(n, carry):
+            re, im = row_block(n), im_block(n)
+            pr, pi, qr, qi = pp[re], pp[im], qq[re], qq[im]
+            gcr, gsr = gc_ref[re, c : c + 1], gs_ref[re, c : c + 1]
+            halves = []
+            for sign, yr, yi in ((0, pr + qi, pi - qr), (1, pr - qi, pi + qr)):
+                at = 2 * c + sign
+                hcr, hsr = hc[at : at + 1], hs[at : at + 1]
+                a = gcr * hcr - gsr * hsr
+                b = gcr * hsr + gsr * hcr
+                halves.append(((yr * a + yi * b).astype(BF), (yi * a - yr * b).astype(BF)))
+            for f in range(facets):
+                if f >= facets // 2:
+                    yr, yi = halves[0]
+                    start = mb * f - half_m
+                else:
+                    yr, yi = halves[1]
+                    start = half_m - mb * (f + 1)
+                ysend[c, f, re] = jnp.concatenate(
+                    [yr[:, start : start + mb], yi[:, start : start + mb]], axis=1
+                )
+            return carry
+
+        lax.fori_loop(0, rows // BLOCK, block, 0, unroll=True)
         copies = [y_copy(c, d) for d in range(1, facets)]
         for copy in copies:
             copy.start()
@@ -277,8 +293,10 @@
             z_copies[c][d - 1].wait_recv()
             total += zrecv[c, d - 1].astype(F32)
         totals.append(total)
-    out_ref[...] = jnp.concatenate(
-        [totals[0][:, :mb], totals[1][:, :mb], totals[0][:, mb:], totals[1][:, mb:]], axis=1
+    out_ref[...] = jnp.transpose(
+        jnp.concatenate(
+            [totals[0][:, :mb], totals[1][:, :mb], totals[0][:, mb:], totals[1][:, mb:]], axis=1
+        )
     )
     for copy in off_copies + y_copies[0] + y_copies[1] + z_copies[0] + z_copies[1]:
         copy.wait_send()
@@ -293,23 +311,29 @@
     rc, rs = (
         np.ascontiguousarray(t.T.astype(np.float32)) for t in half_tables_rows(rows, half_i)
     )
+    padded = -(-rows // LANES) * LANES
     loads = 2 * (half_k // CHUNK) + 6
     dma = pltpu.SemaphoreType.DMA
     flops = 2 * (4 * 2 * rows * half_k * half_m + 4 * half_i * facets * rows * 2 * mb)
     out = pl.pallas_call(
         functools.partial(kernel, facets, strips),
-        out_shape=jax.ShapeDtypeStruct((ib, 4 * mb), F32),
+        out_shape=jax.ShapeDtypeStruct((4 * mb, ib), F32),
         in_specs=[pl.BlockSpec(memory_space=pltpu.HBM)] * 7,
         out_specs=pl.BlockSpec(memory_space=pltpu.VMEM),
         scratch_shapes=[
             pltpu.SMEM((1, 2), jnp.int32),
             pltpu.SMEM((COLUMNS, 2), jnp.int32),
             pltpu.VMEM((2, rows, width), BF),
+            pltpu.VMEM((2 * rows, half_k), BF),
             pltpu.VMEM((half_k, half_m), BF),
             pltpu.VMEM((half_k, half_m), BF),
             pltpu.VMEM((half_i, rows), F32),
             pltpu.VMEM((half_i, rows), F32),
             pltpu.VMEM((COLUMNS, 2, 2 * rows, half_k), BF),
+            pltpu.VMEM((padded, 8), F32),
+            pltpu.VMEM((padded, 8), F32),
+            pltpu.VMEM((2 * rows, half_m), F32),
+            pltpu.VMEM((2 * rows, half_m), F32),
             pltpu.VMEM((COLUMNS, facets, rows, 2 * mb), BF),
             pltpu.VMEM((COLUMNS, facets, rows, 2 * mb), BF),
             pltpu.VMEM((half_i, facets * rows), BF),
@@ -327,13 +351,13 @@
             dma((COLUMNS, strips - 1)),
         ],
         compiler_params=pltpu.CompilerParams(
-            collective_id=0, has_side_effects=True, vmem_limit_bytes=40 * 1024 * 1024
+            collective_id=0, has_side_effects=True, vmem_limit_bytes=63 * 1024 * 1024
         ),
         cost_estimate=pl.CostEstimate(
             flops=flops, bytes_accessed=4 * 1024 * 1024, transcendentals=0
         ),
     )(facet_offsets, subgrid_offsets, facet_pixels, ct, st, rc, rs)
-    return out.reshape(ib, 2, COLUMNS, mb)
+    return jnp.transpose(out.reshape(2, COLUMNS, mb, ib), (3, 0, 1, 2))
 
 
 def half_tables_rows(rows, half_i):

time: 29.2 us -> 23 us (0.79)
  local copies, waits for them, and re-layouts: 7.94 us -> 1.57 us
    unnamed x14 -> x1, local copies, waits for them, and re-layouts: 7.18 us -> 1.57 us
    pallas_call x1 -> x0, local copies, waits for them, and re-layouts: 0.76 us -> none  [per_device(): pl.pallas_call(functools.partial(kernel, facets, strips), out_shape=jax.S...]
where the time goes in v2:
time: 23 us; the launch traced here: 22.7 us
  Pallas kernels  21.1 us (92%)
  local copies, waits for them, and re-layouts  1.57 us (7%)
    pallas_call x1, Pallas kernels, per_device(): pl.pallas_call(functools.partial(kernel, facets, strips), out_shape=jax.S...  21.1 us
    unnamed x1, local copies, waits for them, and re-layouts  1.57 us

profile of v2, /device:TPU:0, one launch (start us, length us, event | category | flops | bytes accessed | tf_op | source)
XLA Modules:
  0.0 22.7 jit_solution(8468967504063855125)
XLA Ops:
  0.0 21.1 %shard_map.73 = f32[256,128]{1,0:T(8,128)} custom-call(s32[1,2]{1,0:T(1,128)} %fo_hbm.1, s32[2,2]{1,0:T(2,128)} %so_hbm.1, bf16[2,1,128,4096]{3,2,1,0:T(8,128)(2,1)} %x_hbm.1, bf16[2048,256]{1,0:T(8,128)(2,1)} %constant.8.clone.ct_hbm, bf16[2048,256]{1,0:T(8,128)(2,1)} %constant.9.clone.st_hbm, f32[256,128]{1,0:T(8,128)} %constant.10.clone.rc_hbm, ...), custom_call_target="tpu_custom_call" | custom-call | flops 1342177280 | bytes 4194304 | tf_op jit(solution)/shard_map/pallas_call | solution.py:318
  21.1 1.6 %copy.9 = f32[128,2,2,64]{0,3,2,1:T(8,128)} copy(f32[128,2,2,64]{0,3,2,1:T(8,128)} %bitcast.3) | data formatting | bytes 262144

commit v3 on v2

--- a/solution.py
+++ b/solution.py
@@ -17,6 +17,7 @@
 LANES = 128
 CHUNK = 256
 BLOCK = 16
+GROUPS = 2
 BF = jnp.bfloat16
 F32 = jnp.float32
 MESH = pl.DeviceIdType.MESH
@@ -80,14 +81,16 @@
 
     fo_load = load(fo_hbm, fo_ref)
     so_load = load(so_hbm, so_ref)
-    x_low, x_high = [], []
-    for j in range(chunks):
-        low = pl.ds((chunks - 1 - j) * CHUNK, CHUNK)
-        high = pl.ds(half_k + j * CHUNK, CHUNK)
-        x_low.append(load(x_hbm.at[:, 0, :, low], x.at[:, :, low]))
-        x_high.append(load(x_hbm.at[:, 0, :, high], x.at[:, :, high]))
-    ct_load = load(ct_hbm, ct)
-    st_load = load(st_hbm, st)
+    x_low, x_high, ct_load, st_load = [], [], [], []
+    for g in range(GROUPS):
+        for j in range(g * chunks // GROUPS, (g + 1) * chunks // GROUPS):
+            low = pl.ds((chunks - 1 - j) * CHUNK, CHUNK)
+            high = pl.ds(half_k + j * CHUNK, CHUNK)
+            x_low.append(load(x_hbm.at[:, 0, :, low], x.at[:, :, low]))
+            x_high.append(load(x_hbm.at[:, 0, :, high], x.at[:, :, high]))
+        span = pl.ds(g * half_k // GROUPS, half_k // GROUPS)
+        ct_load.append(load(ct_hbm.at[span], ct.at[span]))
+        st_load.append(load(st_hbm.at[span], st.at[span]))
     rc_load = load(rc_hbm, rc)
     rs_load = load(rs_hbm, rs)
 
@@ -139,37 +142,53 @@
     def im_block(n):
         return pl.ds(pl.multiple_of(rows + n * BLOCK, BLOCK), BLOCK)
 
-    def phase_column(c):
-        for j in range(chunks):
-            cols = pl.ds(j * CHUNK, CHUNK)
-            high_cols = pl.ds(half_k + j * CHUNK, CHUNK)
+    def column_products(c):
+        per_group = chunks // GROUPS
+        for g in range(GROUPS):
+            group = range(g * per_group, (g + 1) * per_group)
+            span = pl.ds(g * per_group * CHUNK, per_group * CHUNK)
             if c == 0:
-                x_low[j].wait()
-                x_high[j].wait()
-                low = x[:, :, pl.ds((chunks - 1 - j) * CHUNK, CHUNK)].reshape(2 * rows, CHUNK)
-                xr[:, cols] = dot(low, flip).astype(BF)
-            first = j * (CHUNK // LANES)
-            p, q = (
-                jnp.concatenate(
-                    [part[first + n : first + n + 1] for n in range(CHUNK // LANES)], axis=1
-                )
-                for part in pq[c]
+                for j in group:
+                    x_low[j].wait()
+                    x_high[j].wait()
+                for j in group:
+                    low = x[:, :, pl.ds((chunks - 1 - j) * CHUNK, CHUNK)].reshape(2 * rows, CHUNK)
+                    xr[:, pl.ds(j * CHUNK, CHUNK)] = dot(low, flip).astype(BF)
+            for j in group:
+                phase_chunk(c, j)
+            if c == 0:
+                ct_load[g].wait()
+                st_load[g].wait()
+            p_part = dot(evod[c, 0, :, span], ct[span])
+            q_part = dot(evod[c, 1, :, span], st[span])
+            pp[c] = p_part if g == 0 else pp[c] + p_part
+            qq[c] = q_part if g == 0 else qq[c] + q_part
+
+    def phase_chunk(c, j):
+        cols = pl.ds(j * CHUNK, CHUNK)
+        high_cols = pl.ds(half_k + j * CHUNK, CHUNK)
+        first = j * (CHUNK // LANES)
+        p, q = (
+            jnp.concatenate(
+                [part[first + n : first + n + 1] for n in range(CHUNK // LANES)], axis=1
             )
-
-            def block(n, carry):
-                re, im = row_block(n), im_block(n)
-                hr, hi = x[0, re, high_cols].astype(F32), x[1, re, high_cols].astype(F32)
-                lr, li = xr[re, cols].astype(F32), xr[im, cols].astype(F32)
-                er, odr, ei, odi = hr + lr, hr - lr, hi + li, hi - li
-                evod[c, 0, re, cols] = (er * p + odi * q).astype(BF)
-                evod[c, 0, im, cols] = (ei * p - odr * q).astype(BF)
-                evod[c, 1, re, cols] = (odr * p + ei * q).astype(BF)
-                evod[c, 1, im, cols] = (odi * p - er * q).astype(BF)
-                return carry
-
-            lax.fori_loop(0, rows // BLOCK, block, 0, unroll=True)
-
-    phase_column(0)
+            for part in pq[c]
+        )
+
+        def block(n, carry):
+            re, im = row_block(n), im_block(n)
+            hr, hi = x[0, re, high_cols].astype(F32), x[1, re, high_cols].astype(F32)
+            lr, li = xr[re, cols].astype(F32), xr[im, cols].astype(F32)
+            er, odr, ei, odi = hr + lr, hr - lr, hi + li, hi - li
+            evod[c, 0, re, cols] = (er * p + odi * q).astype(BF)
+            evod[c, 0, im, cols] = (ei * p - odr * q).astype(BF)
+            evod[c, 1, re, cols] = (odr * p + ei * q).astype(BF)
+            evod[c, 1, im, cols] = (odi * p - er * q).astype(BF)
+            return carry
+
+        lax.fori_loop(0, rows // BLOCK, block, 0, unroll=True)
+
+    column_products(0)
     pl.semaphore_wait(barrier, facets - 1 + strips - 1)
 
     def off_copy(d):
@@ -209,16 +228,11 @@
     y_copies = []
     for c in range(COLUMNS):
         if c > 0:
-            phase_column(c)
-        else:
-            ct_load.wait()
-            st_load.wait()
-        pp[...] = dot(evod[c, 0], ct[...])
-        qq[...] = dot(evod[c, 1], st[...])
+            column_products(c)
 
         def block(n, carry):
             re, im = row_block(n), im_block(n)
-            pr, pi, qr, qi = pp[re], pp[im], qq[re], qq[im]
+            pr, pi, qr, qi = pp[c, re], pp[c, im], qq[c, re], qq[c, im]
             gcr, gsr = gc_ref[re, c : c + 1], gs_ref[re, c : c + 1]
             halves = []
             for sign, yr, yi in ((0, pr + qi, pi - qr), (1, pr - qi, pi + qr)):
@@ -312,7 +326,7 @@
         np.ascontiguousarray(t.T.astype(np.float32)) for t in half_tables_rows(rows, half_i)
     )
     padded = -(-rows // LANES) * LANES
-    loads = 2 * (half_k // CHUNK) + 6
+    loads = 2 * (half_k // CHUNK) + 2 * GROUPS + 4
     dma = pltpu.SemaphoreType.DMA
     flops = 2 * (4 * 2 * rows * half_k * half_m + 4 * half_i * facets * rows * 2 * mb)
     out = pl.pallas_call(
@@ -332,8 +346,8 @@
             pltpu.VMEM((COLUMNS, 2, 2 * rows, half_k), BF),
             pltpu.VMEM((padded, 8), F32),
             pltpu.VMEM((padded, 8), F32),
-            pltpu.VMEM((2 * rows, half_m), F32),
-            pltpu.VMEM((2 * rows, half_m), F32),
+            pltpu.VMEM((COLUMNS, 2 * rows, half_m), F32),
+            pltpu.VMEM((COLUMNS, 2 * rows, half_m), F32),
             pltpu.VMEM((COLUMNS, facets, rows, 2 * mb), BF),
             pltpu.VMEM((COLUMNS, facets, rows, 2 * mb), BF),
             pltpu.VMEM((half_i, facets * rows), BF),

time: 23 us -> 22.6 us (0.983)
    pallas_call x1, Pallas kernels: 21.1 us -> 20.9 us  [per_device(): pl.pallas_call(functools.partial(kernel, facets, strips), out_shape=jax.S...]
where the time goes in v3:
time: 22.6 us; the launch traced here: 22.4 us
  Pallas kernels  20.9 us (92%)
  local copies, waits for them, and re-layouts  1.57 us (7%)
    pallas_call x1, Pallas kernels, per_device(): pl.pallas_call(functools.partial(kernel, facets, strips), out_shape=jax.S...  20.9 us
    unnamed x1, local copies, waits for them, and re-layouts  1.57 us

profile of v3, /device:TPU:0, one launch (start us, length us, event | category | flops | bytes accessed | tf_op | source)
XLA Modules:
  0.0 22.4 jit_solution(5752206663792930153)
XLA Ops:
  0.0 20.9 %shard_map.73 = f32[256,128]{1,0:T(8,128)} custom-call(s32[1,2]{1,0:T(1,128)} %fo_hbm.1, s32[2,2]{1,0:T(2,128)} %so_hbm.1, bf16[2,1,128,4096]{3,2,1,0:T(8,128)(2,1)} %x_hbm.1, bf16[2048,256]{1,0:T(8,128)(2,1)} %constant.8.clone.ct_hbm, bf16[2048,256]{1,0:T(8,128)(2,1)} %constant.9.clone.st_hbm, f32[256,128]{1,0:T(8,128)} %constant.10.clone.rc_hbm, ...), custom_call_target="tpu_custom_call" | custom-call | flops 1342177280 | bytes 4194304 | tf_op jit(solution)/shard_map/pallas_call | solution.py:332
  20.9 1.6 %copy.9 = f32[128,2,2,64]{0,3,2,1:T(8,128)} copy(f32[128,2,2,64]{0,3,2,1:T(8,128)} %bitcast.3) | data formatting | bytes 262144

commit v4 on v3

--- a/solution.py
+++ b/solution.py
@@ -43,6 +43,23 @@
         c = c * h2 + (-1.0) ** (n // 2) / math.factorial(n)
     s = s * h
     return 1.0 - 2.0 * s * s, 2.0 * s * c
+
+
+def partner(me, d, count):
+    peer, bit = 0, 1
+    while bit < count:
+        digit = me // bit % 2
+        peer = peer + bit * ((1 - digit) if d & bit else digit)
+        bit *= 2
+    return peer
+
+
+def spread_order(count):
+    quarter = count // 4
+    order = []
+    for n in range(quarter):
+        order += [3 * quarter + n, 2 * quarter + n]
+    return order + [d for d in range(2 * quarter - 1, 0, -1)]
 
 
 def iota(shape, dim):
@@ -94,8 +111,8 @@
     rc_load = load(rc_hbm, rc)
     rs_load = load(rs_hbm, rs)
 
-    facet_peers = [lax.rem(f_me + d, facets) for d in range(1, facets)]
-    strip_peers = [lax.rem(s_me + d, strips) for d in range(1, strips)]
+    facet_peers = [partner(f_me, d, facets) for d in range(1, facets)]
+    strip_peers = [partner(s_me, d, strips) for d in range(1, strips)]
     barrier = pltpu.get_barrier_semaphore()
     for peer in facet_peers:
         pl.semaphore_signal(barrier, inc=1, device_id=(peer, s_me), device_id_type=MESH)
@@ -255,8 +272,8 @@
 
         lax.fori_loop(0, rows // BLOCK, block, 0, unroll=True)
         copies = [y_copy(c, d) for d in range(1, facets)]
-        for copy in copies:
-            copy.start()
+        for d in spread_order(facets):
+            copies[d - 1].start()
         y_copies.append(copies)
         yrecv[c, f_me] = ysend[c, f_me]
 
@@ -296,7 +313,7 @@
         z = jnp.concatenate([lower_rows, upper_rows], axis=0)
         zsend[c] = z.reshape(strips, ib, 2 * mb)
         copies = [z_copy(c, d) for d in range(1, strips)]
-        for copy in copies:
+        for copy in reversed(copies):
             copy.start()
         z_copies.append(copies)
 

time: 22.6 us -> 24.6 us (1.088)
  Pallas kernels: 20.9 us -> 22.9 us
    pallas_call x1, Pallas kernels: 20.9 us -> 22.9 us  [per_device(): pl.pallas_call(functools.partial(kernel, facets, strips), out_shape=jax.S...]
where the time goes in v4:
time: 24.6 us; the launch traced here: 24.5 us
  Pallas kernels  22.9 us (93%)
  local copies, waits for them, and re-layouts  1.57 us (6%)
    pallas_call x1, Pallas kernels, per_device(): pl.pallas_call(functools.partial(kernel, facets, strips), out_shape=jax.S...  22.9 us
    unnamed x1, local copies, waits for them, and re-layouts  1.57 us

profile of v4, /device:TPU:0, one launch (start us, length us, event | category | flops | bytes accessed | tf_op | source)
XLA Modules:
  0.0 24.5 jit_solution(4470619204943608225)
XLA Ops:
  0.0 22.9 %shard_map.73 = f32[256,128]{1,0:T(8,128)} custom-call(s32[1,2]{1,0:T(1,128)} %fo_hbm.1, s32[2,2]{1,0:T(2,128)} %so_hbm.1, bf16[2,1,128,4096]{3,2,1,0:T(8,128)(2,1)} %x_hbm.1, bf16[2048,256]{1,0:T(8,128)(2,1)} %constant.8.clone.ct_hbm, bf16[2048,256]{1,0:T(8,128)(2,1)} %constant.9.clone.st_hbm, f32[256,128]{1,0:T(8,128)} %constant.10.clone.rc_hbm, ...), custom_call_target="tpu_custom_call" | custom-call | flops 1342177280 | bytes 4194304 | tf_op jit(solution)/shard_map/pallas_call | solution.py:349
  22.9 1.6 %copy.9 = f32[128,2,2,64]{0,3,2,1:T(8,128)} copy(f32[128,2,2,64]{0,3,2,1:T(8,128)} %bitcast.3) | data formatting | bytes 262144

commit v5 on v3

--- a/solution.py
+++ b/solution.py
@@ -69,7 +69,6 @@
     mb = FREQ // facets
     ib = ROW_FREQ // strips
     chunks = half_k // CHUNK
-    scale = 1.0 / math.sqrt(width * rows * strips * facets)
 
     loads = []
 
@@ -124,7 +123,6 @@
     first = jnp.where(row < 2, u0[0], u0[1])
     freq = first + jnp.where((row & 1) == 0, half_m + lane, half_m - 1 - lane)
     hc, hs = cos_sin((2 * fx + (width - 1)) * freq, 2 * IMAGE_N)
-    hc, hs = hc * scale, hs * scale
 
     padded = -(-rows // LANES) * LANES
     row = iota((8, padded), 0)
@@ -290,11 +288,12 @@
         aa = dot(tc[...], y)
         bb = dot(ts[...], y)
         turned = jnp.concatenate([bb[:, mb:], -bb[:, :mb]], axis=1)
+        half_s = strips // 2
         upper_rows = dot((aa + turned).astype(BF), order).astype(BF)
         lower_rows = dot(flip, (aa - turned).astype(BF)).astype(BF)
         lower_rows = dot(lower_rows, order).astype(BF)
-        z = jnp.concatenate([lower_rows, upper_rows], axis=0)
-        zsend[c] = z.reshape(strips, ib, 2 * mb)
+        zsend[c, half_s:] = upper_rows.reshape(half_s, ib, 2 * mb)
+        zsend[c, :half_s] = lower_rows.reshape(half_s, ib, 2 * mb)
         copies = [z_copy(c, d) for d in range(1, strips)]
         for copy in copies:
             copy.start()
@@ -371,7 +370,8 @@
             flops=flops, bytes_accessed=4 * 1024 * 1024, transcendentals=0
         ),
     )(facet_offsets, subgrid_offsets, facet_pixels, ct, st, rc, rs)
-    return jnp.transpose(out.reshape(2, COLUMNS, mb, ib), (3, 0, 1, 2))
+    scale = 1.0 / math.sqrt(width * rows * strips * facets)
+    return jnp.transpose(scale * out.reshape(2, COLUMNS, mb, ib), (3, 0, 1, 2))
 
 
 def half_tables_rows(rows, half_i):

time: 22.6 us -> 22.6 us (level)
  other arithmetic: 0 us -> 1.57 us
  local copies, waits for them, and re-layouts: 1.57 us -> 0 us
    mul x0 -> x1, other arithmetic: none -> 1.57 us  [per_device(): return jnp.transpose(scale * out.reshape(2, COLUMNS, mb, ib), (3, 0, 1, 2))]
    unnamed x1 -> x0, local copies, waits for them, and re-layouts: 1.57 us -> none
where the time goes in v5:
time: 22.6 us; the launch traced here: 22.4 us
  Pallas kernels  20.9 us (92%)
  other arithmetic  1.57 us (7%)
    pallas_call x1, Pallas kernels, per_device(): pl.pallas_call(functools.partial(kernel, facets, strips), out_shape=jax.S...  20.9 us
    mul x1, other arithmetic, per_device(): return jnp.transpose(scale * out.reshape(2, COLUMNS, mb, ib), (3, 0, 1, 2))  1.57 us

profile of v5, /device:TPU:0, one launch (start us, length us, event | category | flops | bytes accessed | tf_op | source)
XLA Modules:
  0.0 22.4 jit_solution(58753740251184105)
XLA Ops:
  0.0 20.9 %shard_map.73 = f32[256,128]{1,0:T(8,128)} custom-call(s32[1,2]{1,0:T(1,128)} %fo_hbm.1, s32[2,2]{1,0:T(2,128)} %so_hbm.1, bf16[2,1,128,4096]{3,2,1,0:T(8,128)(2,1)} %x_hbm.1, bf16[2048,256]{1,0:T(8,128)(2,1)} %constant.10.clone.ct_hbm, bf16[2048,256]{1,0:T(8,128)(2,1)} %constant.11.clone.st_hbm, f32[256,128]{1,0:T(8,128)} %constant.12.clone.rc_hbm, ...), custom_call_target="tpu_custom_call" | custom-call | flops 1342177280 | bytes 4194304 | tf_op jit(solution)/shard_map/pallas_call | solution.py:331
  20.9 1.6 %broadcast_multiply_fusion = f32[256,128]{1,0:T(8,128)} fusion(f32[256,128]{1,0:T(8,128)} %shard_map.73), kind=kLoop, calls=%fused_computation | loop fusion | flops 32768 | bytes 262144 | tf_op jit(solution)/shard_map/mul | solution.py:374
